TPU v7x, 128 devices: a whole 4x4x4 slice. The times are simulated.
128 devices in a mesh: row: 8 (over y, x_hi), col: 16 (over x_lo, z, core).
Axes of the slice: x: 4 (x_hi: 2, x_lo: 2; x = x_hi * 2 + x_lo), y: 4, z: 4, core: 2. Of those that a mesh axis runs over, the one named last changes fastest.
Arguments:
- amplitudes: float32 [64, 131072], P(None, ('row', 'col')), may hold values from -6 to 6
- ladder_ints: float32 [131072, 4096], P('row', 'col'), may hold values from -0.046875 to 0.046875
- tile_mask: int32 [2048, 64], replicated, may hold values from 0 to 1, as said below
Outputs:
- ladder: float32 [64, 4096], P(None, 'col')
Inputs may be any that keep to these rules, and one draw needn't show every extreme that they name: `tile_mask`: among each aligned run of 16 cd tile rows (one device's amplitude tiles), at most 8 rows hold a nonzero tile.
All inputs are finite; a program needn't handle non-finite values.
Results may differ from a plain program's by a relative error of at most 0.0001.
Values sent between devices are 32-bit elements; how exact they have to be, the bound alone decides.
A program may use at most 192 MiB of HBM per device.

v0:
```python
import jax
import jax.numpy as jnp
from jax import lax
from jax.sharding import PartitionSpec as P

TILE = 64


def per_device(amplitudes, ladder_ints, tile_mask):
    ab_width = ladder_ints.shape[1]
    row_tiles = ladder_ints.shape[0] // TILE
    ab_tiles = ab_width // TILE
    row_id = lax.axis_index("row")
    col_id = lax.axis_index("col")
    my_mask = lax.dynamic_slice(
        tile_mask, (row_id * row_tiles, col_id * ab_tiles), (row_tiles, ab_tiles)
    )
    masked = (
        ladder_ints.reshape(row_tiles, TILE, ab_tiles, TILE)
        * my_mask[:, None, :, None].astype(jnp.float32)
    ).reshape(ladder_ints.shape)
    partial_sum = jnp.dot(
        lax.all_gather(amplitudes, "col", axis=1, tiled=True),
        masked,
        precision=lax.Precision.HIGHEST,
        preferred_element_type=jnp.float32,
    )
    return lax.psum(partial_sum, "row")


def solution(mesh):
    in_specs = (P(None, ("row", "col")), P("row", "col"), P())
    out_specs = P(None, "col")
    return jax.shard_map(
        per_device, mesh=mesh, in_specs=in_specs, out_specs=out_specs, check_vma=False
    )
```

profile of v0, /device:TPU:0, one launch (start us, length us, event | category | flops | bytes accessed | tf_op | source)
XLA Modules:
  0.0 178.5 jit_solution(2918529948657118630)
XLA Ops:
  6.5 0.0 all-gather.2.cloned.1.call-start
  6.5 0.7 all-gather.2.cloned.1.call-update
  7.3 0.0 all-reduce.2.cloned.1.call-start
  7.3 0.8 dynamic-slice_convert_fusion
  8.1 11.3 %mul.19 = f32[256,64,4,64]{1,0,3,2:T(8,128)} broadcast(f32[256,4]{0,1:T(4,128)S(1)} %dynamic-slice_convert_fusion), dimensions={0,2} | broadcast | bytes 16781312 | tf_op jit(solution)/shard_map/mul | solution.py:19
  19.4 25.1 %mul.20 = f32[16384,256]{0,1:T(8,128)} reshape(f32[256,64,4,64]{1,0,3,2:T(8,128)} %mul.19) | data formatting | bytes 33554432 | tf_op jit(solution)/shard_map/mul | solution.py:19
  44.5 17.4 %copy.5 = f32[16384,256]{0,1:T(8,128)} copy(f32[16384,256]{1,0:T(8,128)} %param.4) | data formatting | bytes 33554432 | tf_op args[1]
  61.9 0.0 all-gather.2.cloned.1.call-done
  61.9 22.5 %fusion.2 = f32[64,256]{1,0:T(8,128)} fusion(f32[64,16384]{1,0:T(8,128)} %all-gather.2.cloned.1.call-done, f32[16384,256]{0,1:T(8,128)} %copy.5, f32[16384,256]{0,1:T(8,128)} %mul.20), kind=kOutput, calls=%fused_computation.2 | convolution fusion | flops 3225419776 | bytes 37814272 | tf_op jit(solution)/shard_map/dot_general | solution.py:22
  84.4 0.0 all-reduce.2.cloned.1.call-update
  84.4 85.8 %all-reduce.2.cloned.1.call-done = f32[64,256]{1,0:T(8,128)} async-done(((f32[64,256]{1,0:T(8,128)}), f32[64,256]{1,0:T(8,128)}) %all-reduce.2.cloned.1.call-update) | async-done | bytes 65552 | tf_op jit(solution)/shard_map/psum | solution.py:28
  170.2 1.5 copy.7
Async XLA Ops:
  6.5 55.4 %all-gather.2.cloned.1.call-start = ((), (), s32[]{:S(2)}) async-start(), calls=%async_computation | async-start | bytes 4456448 | tf_op jit(solution)/shard_map/all_gather | solution.py:23
  7.3 162.9 %all-reduce.2.cloned.1.call-start = ((), (), s32[]{:S(2)}) async-start(), calls=%async_computation.1 | async-start | bytes 131072 | tf_op jit(solution)/shard_map/psum | solution.py:28
Sparse Core Ops, SparseCore 0:
  9.0 39.8 all-gather.1
  84.5 85.5 all-reduce.1
where the time goes:
time: 179 us; the launch traced here: 178 us
  waiting for transfers between devices  86.5 us (48%)
  local copies, waits for them, and re-layouts  55.3 us (31%)
  matrix products  22.5 us (13%)
  between operations  13.4 us (7%)
    psum x1, waiting for transfers between devices, per_device(): return lax.psum(partial_sum, 'row')  85.8 us
    mul x2, local copies, waits for them, and re-layouts, per_device(): ladder_ints.reshape(row_tiles, TILE, ab_tiles, TILE)  36.4 us
    dot_general x1, matrix products, per_device(): jnp.dot(lax.all_gather(amplitudes, 'col', axis=1, tiled=True), masked, pr...  22.5 us
    unnamed x2, local copies, waits for them, and re-layouts  18.9 us
  transfers between devices with their start and end apart: 2, of which 1 were waited for; matrix products, arithmetic and copies ran while one was open for 31% of the time, Pallas kernels for 0%

commit v1 on v0

v1 whole, which is shorter than its diff:
```python
import functools

import jax
import jax.numpy as jnp
from jax import lax
from jax.experimental import pallas as pl
from jax.experimental.pallas import tpu as pltpu
from jax.sharding import PartitionSpec as P

TILE = 64
GROUP = 16
LIVE = 8
PIECES = 4
LANES = 128
MESH = pl.DeviceIdType.MESH

TREE_A = {(0, 0): "udx", (0, 1): "ux", (1, 0): "d", (1, 1): "u"}
TREE_M = {(0, 0): "udx", (0, 3): "dx", (1, 0): "u", (1, 3): "d"}
TREES = (TREE_A, TREE_M, TREE_A, TREE_M)

ROUNDS = (((0, 1), (0, 3), (1, 0)), ((0, 2), (1, 1), (1, 3)), ((1, 2),))


def kernel(rows, t_hbm, v_hbm, m_hbm, o_ref, t_in, m_in, list_v, list_s, v_hi, v_lo, t_all, acc, red, fin,
           in_sem, v_sem, out_sem, got_sem, red_out, red_got, fin_out, fin_got, *v_in):
    row = lax.axis_index("row")
    col = lax.axis_index("col")
    core = lax.rem(col, 2)
    z = lax.rem(lax.div(col, 2), 4)
    x_lo = lax.div(col, 8)

    def col_of(dx, dz, dc):
        return lax.rem(x_lo + dx, 2) * 8 + lax.rem(z + dz, 4) * 2 + lax.rem(core + dc, 2)

    link = {"u": col_of(0, 1, 0), "d": col_of(0, 3, 0), "x": col_of(1, 0, 0), "s": col_of(0, 0, 1)}

    mask_copy = pltpu.make_async_copy(
        m_hbm.at[:, pl.ds(pl.multiple_of(row * 256, 256), 256)], m_in, in_sem.at[0])
    mask_copy.start()
    t_copy = pltpu.make_async_copy(t_hbm, t_in, in_sem.at[1])
    t_copy.start()

    order = [(0, 0)] + [e for rnd in ROUNDS for e in rnd]
    owner = {(e, dc): col_of(e[0], (4 - e[1]) % 4, dc) for e in order for dc in (0, 1)}
    v_of = dict(zip(owner, v_in))
    v_copies = {}
    for n, at in enumerate(owner):
        v_copies[at] = pltpu.make_async_copy(
            v_hbm.at[pl.ds(pl.multiple_of(owner[at] * 1024, 1024), 1024), :], v_of[at], v_sem.at[n])
        v_copies[at].start()

    barrier = pltpu.get_barrier_semaphore()
    for to in link.values():
        pl.semaphore_signal(barrier, inc=1, device_id={"col": to}, device_id_type=MESH)
    for k in range(1, rows):
        pl.semaphore_signal(barrier, inc=1, device_id={"row": lax.rem(row + k, rows)}, device_id_type=MESH)

    mask_copy.wait()
    live = jnp.broadcast_to(jnp.max(m_in[...], axis=0, keepdims=True), (8, 256))
    lane = lax.broadcasted_iota(jnp.int32, (8, 256), 1)
    slot = lax.broadcasted_iota(jnp.int32, (8, 256), 0)
    tile = lane & 15
    count = live
    for s in (1, 2, 4, 8):
        count = count + jnp.where(tile >= s, pltpu.roll(count, s, 1), 0)
    place = jnp.where(live > 0, count - 1, 15 - tile + count)
    mine = m_in[pl.ds(pl.multiple_of(lax.div(col, 2) * 8, 8), 8), :]
    bit = slot - lax.rem(col, 2) * 4
    weight = jnp.where(bit == 0, 16, jnp.where(bit == 1, 32, jnp.where(bit == 2, 64, jnp.where(bit == 3, 128, 0))))
    code = jnp.sum(mine * weight, axis=0, keepdims=True)
    entry = jnp.where(place == slot, tile + code, 0)
    for s in (1, 2, 4, 8):
        entry = entry + pltpu.roll(entry, 256 - s, 1)
    list_v[...] = entry
    list_copy = pltpu.make_async_copy(list_v, list_s, in_sem.at[2])
    list_copy.start()
    list_copy.wait()
    t_copy.wait()

    left = lax.broadcasted_iota(jnp.int32, (TILE, LANES), 1) < TILE
    for p in range(PIECES):
        halves = []
        for h in (0, 1):
            at = list_s[2 * p + h, col * GROUP] & 15
            block = t_in[:, pl.ds((at >> 1) * LANES, LANES)]
            odd = jnp.full((TILE, LANES), at, jnp.int32) & 1
            halves.append(jnp.where(odd != h, pltpu.roll(block, TILE, 1), block))
        t_all[col, p] = jnp.where(left, halves[0], halves[1])

    pl.semaphore_wait(barrier, len(link) + rows - 1)

    sent = []

    def piece(s, p, to, n):
        return pltpu.make_async_remote_copy(
            src_ref=t_all.at[s, p], dst_ref=t_all.at[s, p], send_sem=out_sem.at[n],
            recv_sem=got_sem.at[s * PIECES + p], device_id={"col": to}, device_id_type=MESH)

    def send(s, p, to):
        copy = piece(s, p, to, len(sent))
        copy.start()
        sent.append(copy)

    def arrive(s, p):
        piece(s, p, link["s"], 0).wait_recv()

    for p in range(PIECES):
        for way in TREES[p][0, 0]:
            send(col, p, link[way])
    for p in range(PIECES):
        send(col, p, link["s"])

    bits = 16 << lax.div(lax.broadcasted_iota(jnp.int32, (1, 256), 1), TILE)

    def prepare(e, dc):
        s = owner[e, dc]
        v_copies[e, dc].wait()

        def one(k, carry):
            at = list_s[k, s * GROUP]
            tile_rows = v_of[e, dc][pl.ds((at & 15) * TILE, TILE), :]
            tile_rows = jnp.where((jnp.full((1, 256), at, jnp.int32) & bits) != 0, tile_rows, 0.0)
            high = tile_rows.astype(jnp.bfloat16)
            low = (tile_rows - high.astype(jnp.float32)).astype(jnp.bfloat16)
            to = pl.ds(pl.multiple_of(k * TILE, TILE), TILE)
            v_hi[s, to, :] = high
            v_lo[s, to, :] = low
            return carry

        lax.fori_loop(0, LIVE, one, 0)

    def multiply(e, dc):
        s = owner[e, dc]
        t = jnp.concatenate([t_all[s, p] for p in range(PIECES)], axis=1)
        high = t.astype(jnp.bfloat16)
        low = (t - high.astype(jnp.float32)).astype(jnp.bfloat16)
        both = jnp.dot(jnp.concatenate([high, low], axis=0), v_hi[s], preferred_element_type=jnp.float32)
        more = jnp.dot(high, v_lo[s], preferred_element_type=jnp.float32)
        acc[...] += both[:64] + (both[64:] + more)

    acc[...] = jnp.zeros_like(acc)
    prepare((0, 0), 0)
    prepare((0, 0), 1)
    multiply((0, 0), 0)

    last = ((0, 0),)
    for rnd in ROUNDS:
        for p in range(PIECES):
            for e in rnd:
                s = owner[e, 0]
                arrive(s, p)
                for way in TREES[p].get(e, ""):
                    send(s, p, link[way])
                send(s, p, link["s"])
            if p < len(rnd):
                prepare(rnd[p], 0)
                prepare(rnd[p], 1)
        for e in last:
            for p in range(PIECES):
                arrive(owner[e, 1], p)
            multiply(e, 1)
        for e in rnd:
            multiply(e, 0)
        last = rnd
    for e in last:
        for p in range(PIECES):
            arrive(owner[e, 1], p)
        multiply(e, 1)

    def part(q):
        return pl.ds(pl.multiple_of(q * 8, 8), 8)

    red_copies, fin_copies = [], []
    for k in range(1, rows):
        to = lax.rem(row + k, rows)
        copy = pltpu.make_async_remote_copy(
            src_ref=acc.at[part(to)], dst_ref=red.at[k], send_sem=red_out.at[k], recv_sem=red_got.at[k],
            device_id={"row": to}, device_id_type=MESH)
        copy.start()
        red_copies.append(copy)
    total = acc[part(row), :]
    for copy in red_copies:
        copy.wait_recv()
    for k in range(1, rows):
        total = total + red[k]
    fin[row] = total
    for k in range(1, rows):
        to = lax.rem(row + k, rows)
        copy = pltpu.make_async_remote_copy(
            src_ref=fin.at[row], dst_ref=fin.at[row], send_sem=fin_out.at[k], recv_sem=fin_got.at[row],
            device_id={"row": to}, device_id_type=MESH)
        copy.start()
        fin_copies.append(copy)
    o_ref[part(row), :] = total
    for k in range(1, rows):
        q = lax.rem(row + k, rows)
        pltpu.make_async_remote_copy(
            src_ref=fin.at[q], dst_ref=fin.at[q], send_sem=fin_out.at[k], recv_sem=fin_got.at[q],
            device_id={"row": q}, device_id_type=MESH).wait_recv()
        o_ref[part(q), :] = fin[q]

    for copy in sent + red_copies + fin_copies:
        copy.wait_send()


def per_device(rows, amplitudes, ladder_ints, tile_mask):
    n_sent = sum(len(ways) for tree in TREES for ways in tree.values()) + 8 * PIECES
    return pl.pallas_call(
        functools.partial(kernel, rows),
        out_shape=jax.ShapeDtypeStruct((64, 256), jnp.float32),
        in_specs=[pl.BlockSpec(memory_space=pl.ANY)] * 3,
        out_specs=pl.BlockSpec(memory_space=pltpu.VMEM),
        scratch_shapes=[
            pltpu.VMEM((64, 1024), jnp.float32),
            pltpu.VMEM((64, 256), jnp.int32),
            pltpu.VMEM((8, 256), jnp.int32),
            pltpu.SMEM((8, 256), jnp.int32),
            pltpu.VMEM((16, LIVE * TILE, 256), jnp.bfloat16),
            pltpu.VMEM((16, LIVE * TILE, 256), jnp.bfloat16),
            pltpu.VMEM((16, PIECES, 64, LANES), jnp.float32),
            pltpu.VMEM((64, 256), jnp.float32),
            pltpu.VMEM((rows, 8, 256), jnp.float32),
            pltpu.VMEM((rows, 8, 256), jnp.float32),
            pltpu.SemaphoreType.DMA((3,)),
            pltpu.SemaphoreType.DMA((16,)),
            pltpu.SemaphoreType.DMA((n_sent,)),
            pltpu.SemaphoreType.DMA((16 * PIECES,)),
            pltpu.SemaphoreType.DMA((rows,)),
            pltpu.SemaphoreType.DMA((rows,)),
            pltpu.SemaphoreType.DMA((rows,)),
            pltpu.SemaphoreType.DMA((rows,)),
        ] + [pltpu.VMEM((1024, 256), jnp.float32)] * 16,
        compiler_params=pltpu.CompilerParams(
            collective_id=0, has_side_effects=True, vmem_limit_bytes=60 * 1024 * 1024),
    )(amplitudes, ladder_ints, tile_mask.T)


def solution(mesh):
    in_specs = (P(None, ("row", "col")), P("row", "col"), P())
    out_specs = P(None, "col")
    return jax.shard_map(
        functools.partial(per_device, mesh.shape["row"]), mesh=mesh, in_specs=in_specs, out_specs=out_specs,
        check_vma=False)
```

time: 179 us -> 36.8 us (0.21)
  waiting for transfers between devices: 86.5 us -> 0 us
  local copies, waits for them, and re-layouts: 55.3 us -> 1.47 us
  Pallas kernels: 0 us -> 35 us
  matrix products: 22.5 us -> 0 us
  between operations: 13.4 us -> 0.01 us
    psum x1 -> x0, waiting for transfers between devices: 85.8 us -> none  [per_device(): return lax.psum(partial_sum, 'row')]
    mul x2 -> x0, local copies, waits for them, and re-layouts: 36.4 us -> none  [per_device(): ladder_ints.reshape(row_tiles, TILE, ab_tiles, TILE)]
    pallas_call x0 -> x1, Pallas kernels: none -> 35 us  [per_device(): pl.pallas_call(functools.partial(kernel, rows), out_shape=jax.ShapeDtypeS...]
    dot_general x1 -> x0, matrix products: 22.5 us -> none  [per_device(): jnp.dot(lax.all_gather(amplitudes, 'col', axis=1, tiled=True), masked, pr...]
    unnamed x2 -> x1, local copies, waits for them, and re-layouts: 18.9 us -> 1.47 us
  transfers between devices with their start and end apart: 2 -> 0, of which waited for: 1 -> 0; matrix products, arithmetic and copies ran while one was open for 31% -> 0% of each run, Pallas kernels for 0% -> 0%
where the time goes in v1:
time: 36.8 us; the launch traced here: 36.5 us
  Pallas kernels  35 us (95%)
  local copies, waits for them, and re-layouts  1.47 us (4%)
    pallas_call x1, Pallas kernels, per_device(): pl.pallas_call(functools.partial(kernel, rows), out_shape=jax.ShapeDtypeS...  35 us
    unnamed x1, local copies, waits for them, and re-layouts  1.47 us

profile of v1, /device:TPU:0, one launch (start us, length us, event | category | flops | bytes accessed | tf_op | source)
XLA Modules:
  0.0 36.5 jit_solution(4983556748809417058)
XLA Ops:
  0.0 35.0 %shard_map.37 = f32[64,256]{1,0:T(8,128)} custom-call(f32[64,1024]{1,0:T(8,128)} %t_hbm.1, f32[16384,256]{1,0:T(8,128)} %v_hbm.1, s32[64,2048]{1,0:T(8,128)} %bitcast.1), custom_call_target="tpu_custom_call" | custom-call | tf_op jit(solution)/shard_map/pallas_call | solution.py:208
  35.0 1.5 %copy.5 = f32[64,256]{1,0:T(8,128)} copy(f32[64,256]{1,0:T(8,128)} %shard_map.37) | data formatting | bytes 131072

commit v2 on v1

--- a/solution.py
+++ b/solution.py
@@ -10,29 +10,37 @@
 TILE = 64
 GROUP = 16
 LIVE = 8
-PIECES = 4
-LANES = 128
+PIECES = 2
+WIDTH = 256
 MESH = pl.DeviceIdType.MESH
 
-TREE_A = {(0, 0): "udx", (0, 1): "ux", (1, 0): "d", (1, 1): "u"}
-TREE_M = {(0, 0): "udx", (0, 3): "dx", (1, 0): "u", (1, 3): "d"}
-TREES = (TREE_A, TREE_M, TREE_A, TREE_M)
-
-ROUNDS = (((0, 1), (0, 3), (1, 0)), ((0, 2), (1, 1), (1, 3)), ((1, 2),))
+TREE = {(0, 1): "xs", (0, 3): "xs", (1, 0): "2s", (0, 2): "s", (1, 1): "s", (1, 3): "s", (1, 2): "s"}
+FIRST = ((1, 0), (0, 1), (0, 3))
+SECOND = ((1, 1), (1, 3), (1, 2))
+ORDER = ((0, 0),) + FIRST + ((0, 2),) + SECOND
+N_SENT = (4 + 1 + 3 + 7) * PIECES
+ROUNDS = 3
 
 
 def kernel(rows, t_hbm, v_hbm, m_hbm, o_ref, t_in, m_in, list_v, list_s, v_hi, v_lo, t_all, acc, red, fin,
-           in_sem, v_sem, out_sem, got_sem, red_out, red_got, fin_out, fin_got, *v_in):
+           in_sem, v_sem, out_sem, got_sem, red_out, red_got, fin_out, fin_got, near_sem, *v_in):
     row = lax.axis_index("row")
     col = lax.axis_index("col")
     core = lax.rem(col, 2)
     z = lax.rem(lax.div(col, 2), 4)
     x_lo = lax.div(col, 8)
+    y = lax.div(row, 2)
+    x_hi = lax.rem(row, 2)
 
     def col_of(dx, dz, dc):
         return lax.rem(x_lo + dx, 2) * 8 + lax.rem(z + dz, 4) * 2 + lax.rem(core + dc, 2)
 
-    link = {"u": col_of(0, 1, 0), "d": col_of(0, 3, 0), "x": col_of(1, 0, 0), "s": col_of(0, 0, 1)}
+    def row_of(dy, dx):
+        return lax.rem(y + dy, 4) * 2 + lax.rem(x_hi + dx, 2)
+
+    link = {"u": col_of(0, 1, 0), "d": col_of(0, 3, 0), "2": col_of(0, 2, 0), "x": col_of(1, 0, 0),
+            "s": col_of(0, 0, 1)}
+    near = ({"row": row_of(1, 0)}, {"row": row_of(3, 0)}, {"col": link["x"]}, {"row": row_of(0, 1), "col": link["x"]})
 
     mask_copy = pltpu.make_async_copy(
         m_hbm.at[:, pl.ds(pl.multiple_of(row * 256, 256), 256)], m_in, in_sem.at[0])
@@ -40,20 +48,17 @@
     t_copy = pltpu.make_async_copy(t_hbm, t_in, in_sem.at[1])
     t_copy.start()
 
-    order = [(0, 0)] + [e for rnd in ROUNDS for e in rnd]
-    owner = {(e, dc): col_of(e[0], (4 - e[1]) % 4, dc) for e in order for dc in (0, 1)}
+    barrier = pltpu.get_barrier_semaphore()
+    for to in [{"col": link[way]} for way in "ud2s"] + list(near):
+        pl.semaphore_signal(barrier, inc=1, device_id=to, device_id_type=MESH)
+
+    owner = {(e, dc): col_of(e[0], (4 - e[1]) % 4, dc) for e in ORDER for dc in (0, 1)}
     v_of = dict(zip(owner, v_in))
     v_copies = {}
     for n, at in enumerate(owner):
         v_copies[at] = pltpu.make_async_copy(
             v_hbm.at[pl.ds(pl.multiple_of(owner[at] * 1024, 1024), 1024), :], v_of[at], v_sem.at[n])
         v_copies[at].start()
-
-    barrier = pltpu.get_barrier_semaphore()
-    for to in link.values():
-        pl.semaphore_signal(barrier, inc=1, device_id={"col": to}, device_id_type=MESH)
-    for k in range(1, rows):
-        pl.semaphore_signal(barrier, inc=1, device_id={"row": lax.rem(row + k, rows)}, device_id_type=MESH)
 
     mask_copy.wait()
     live = jnp.broadcast_to(jnp.max(m_in[...], axis=0, keepdims=True), (8, 256))
@@ -77,17 +82,17 @@
     list_copy.wait()
     t_copy.wait()
 
-    left = lax.broadcasted_iota(jnp.int32, (TILE, LANES), 1) < TILE
-    for p in range(PIECES):
+    left = lax.broadcasted_iota(jnp.int32, (64, 128), 1) < TILE
+    for p in range(LIVE // 2):
         halves = []
         for h in (0, 1):
             at = list_s[2 * p + h, col * GROUP] & 15
-            block = t_in[:, pl.ds((at >> 1) * LANES, LANES)]
-            odd = jnp.full((TILE, LANES), at, jnp.int32) & 1
+            block = t_in[:, pl.ds((at >> 1) * 128, 128)]
+            odd = jnp.full((64, 128), at, jnp.int32) & 1
             halves.append(jnp.where(odd != h, pltpu.roll(block, TILE, 1), block))
-        t_all[col, p] = jnp.where(left, halves[0], halves[1])
-
-    pl.semaphore_wait(barrier, len(link) + rows - 1)
+        t_all[col, p // 2, :, (p % 2) * 128:(p % 2) * 128 + 128] = jnp.where(left, halves[0], halves[1])
+
+    pl.semaphore_wait(barrier, 8)
 
     sent = []
 
@@ -96,19 +101,28 @@
             src_ref=t_all.at[s, p], dst_ref=t_all.at[s, p], send_sem=out_sem.at[n],
             recv_sem=got_sem.at[s * PIECES + p], device_id={"col": to}, device_id_type=MESH)
 
-    def send(s, p, to):
-        copy = piece(s, p, to, len(sent))
-        copy.start()
-        sent.append(copy)
-
-    def arrive(s, p):
-        piece(s, p, link["s"], 0).wait_recv()
-
-    for p in range(PIECES):
-        for way in TREES[p][0, 0]:
-            send(col, p, link[way])
-    for p in range(PIECES):
-        send(col, p, link["s"])
+    def send(s, p, ways):
+        for way in ways:
+            copy = piece(s, p, link[way], len(sent))
+            copy.start()
+            sent.append(copy)
+
+    def arrive(e, dc, p):
+        piece(owner[e, dc], p, link["s"], 0).wait_recv()
+
+    for p in range(PIECES):
+        send(col, p, "udx")
+    for p in range(PIECES):
+        send(col, p, "s2")
+
+    def tell(n):
+        for to in near:
+            pl.semaphore_signal(near_sem.at[n], inc=1, device_id=to, device_id_type=MESH)
+
+    def hear(n):
+        pl.semaphore_wait(near_sem.at[n], len(near))
+
+    tell(0)
 
     bits = 16 << lax.div(lax.broadcasted_iota(jnp.int32, (1, 256), 1), TILE)
 
@@ -138,34 +152,52 @@
         more = jnp.dot(high, v_lo[s], preferred_element_type=jnp.float32)
         acc[...] += both[:64] + (both[64:] + more)
 
+    def pass_on(e, p):
+        arrive(e, 0, p)
+        send(owner[e, 0], p, TREE[e])
+
+    def sibling(e):
+        for p in range(PIECES):
+            arrive(e, 1, p)
+        multiply(e, 1)
+
     acc[...] = jnp.zeros_like(acc)
     prepare((0, 0), 0)
     prepare((0, 0), 1)
     multiply((0, 0), 0)
-
-    last = ((0, 0),)
-    for rnd in ROUNDS:
-        for p in range(PIECES):
-            for e in rnd:
-                s = owner[e, 0]
-                arrive(s, p)
-                for way in TREES[p].get(e, ""):
-                    send(s, p, link[way])
-                send(s, p, link["s"])
-            if p < len(rnd):
-                prepare(rnd[p], 0)
-                prepare(rnd[p], 1)
-        for e in last:
-            for p in range(PIECES):
-                arrive(owner[e, 1], p)
-            multiply(e, 1)
-        for e in rnd:
-            multiply(e, 0)
-        last = rnd
-    for e in last:
-        for p in range(PIECES):
-            arrive(owner[e, 1], p)
-        multiply(e, 1)
+    sibling((0, 0))
+    for e in FIRST:
+        prepare(e, 0)
+        prepare(e, 1)
+    hear(0)
+    tell(1)
+    for p in range(PIECES):
+        for e in FIRST:
+            pass_on(e, p)
+    for e in ((0, 2),) + SECOND[:2]:
+        prepare(e, 0)
+        prepare(e, 1)
+    for p in range(PIECES):
+        pass_on((0, 2), p)
+    hear(1)
+    tell(2)
+    for e in FIRST:
+        multiply(e, 0)
+    for e in SECOND[2:]:
+        prepare(e, 0)
+        prepare(e, 1)
+    for e in FIRST:
+        sibling(e)
+    multiply((0, 2), 0)
+    hear(2)
+    for p in range(PIECES):
+        for e in SECOND:
+            pass_on(e, p)
+    sibling((0, 2))
+    for e in SECOND:
+        multiply(e, 0)
+    for e in SECOND:
+        sibling(e)
 
     def part(q):
         return pl.ds(pl.multiple_of(q * 8, 8), 8)
@@ -204,7 +236,6 @@
 
 
 def per_device(rows, amplitudes, ladder_ints, tile_mask):
-    n_sent = sum(len(ways) for tree in TREES for ways in tree.values()) + 8 * PIECES
     return pl.pallas_call(
         functools.partial(kernel, rows),
         out_shape=jax.ShapeDtypeStruct((64, 256), jnp.float32),
@@ -217,18 +248,19 @@
             pltpu.SMEM((8, 256), jnp.int32),
             pltpu.VMEM((16, LIVE * TILE, 256), jnp.bfloat16),
             pltpu.VMEM((16, LIVE * TILE, 256), jnp.bfloat16),
-            pltpu.VMEM((16, PIECES, 64, LANES), jnp.float32),
+            pltpu.VMEM((16, PIECES, 64, WIDTH), jnp.float32),
             pltpu.VMEM((64, 256), jnp.float32),
             pltpu.VMEM((rows, 8, 256), jnp.float32),
             pltpu.VMEM((rows, 8, 256), jnp.float32),
             pltpu.SemaphoreType.DMA((3,)),
             pltpu.SemaphoreType.DMA((16,)),
-            pltpu.SemaphoreType.DMA((n_sent,)),
+            pltpu.SemaphoreType.DMA((N_SENT,)),
             pltpu.SemaphoreType.DMA((16 * PIECES,)),
             pltpu.SemaphoreType.DMA((rows,)),
             pltpu.SemaphoreType.DMA((rows,)),
             pltpu.SemaphoreType.DMA((rows,)),
             pltpu.SemaphoreType.DMA((rows,)),
+            pltpu.SemaphoreType.REGULAR((ROUNDS,)),
         ] + [pltpu.VMEM((1024, 256), jnp.float32)] * 16,
         compiler_params=pltpu.CompilerParams(
             collective_id=0, has_side_effects=True, vmem_limit_bytes=60 * 1024 * 1024),

time: 36.8 us -> 35.1 us (0.954)
  Pallas kernels: 35 us -> 33.4 us
    pallas_call x1, Pallas kernels: 35 us -> 33.4 us  [per_device(): pl.pallas_call(functools.partial(kernel, rows), out_shape=jax.ShapeDtypeS...]
where the time goes in v2:
time: 35.1 us; the launch traced here: 34.9 us
  Pallas kernels  33.4 us (95%)
  local copies, waits for them, and re-layouts  1.47 us (4%)
    pallas_call x1, Pallas kernels, per_device(): pl.pallas_call(functools.partial(kernel, rows), out_shape=jax.ShapeDtypeS...  33.4 us
    unnamed x1, local copies, waits for them, and re-layouts  1.47 us

profile of v2, /device:TPU:0, one launch (start us, length us, event | category | flops | bytes accessed | tf_op | source)
XLA Modules:
  0.0 34.9 jit_solution(11844162635260035528)
XLA Ops:
  0.0 33.4 %shard_map.37 = f32[64,256]{1,0:T(8,128)} custom-call(f32[64,1024]{1,0:T(8,128)} %t_hbm.1, f32[16384,256]{1,0:T(8,128)} %v_hbm.1, s32[64,2048]{1,0:T(8,128)} %bitcast.1), custom_call_target="tpu_custom_call" | custom-call | tf_op jit(solution)/shard_map/pallas_call | solution.py:239
  33.5 1.5 %copy.5 = f32[64,256]{1,0:T(8,128)} copy(f32[64,256]{1,0:T(8,128)} %shard_map.37) | data formatting | bytes 131072

commit v3 on v2

--- a/solution.py
+++ b/solution.py
@@ -15,7 +15,7 @@
 MESH = pl.DeviceIdType.MESH
 
 TREE = {(0, 1): "xs", (0, 3): "xs", (1, 0): "2s", (0, 2): "s", (1, 1): "s", (1, 3): "s", (1, 2): "s"}
-FIRST = ((1, 0), (0, 1), (0, 3))
+FIRST = ((0, 1), (0, 3), (1, 0))
 SECOND = ((1, 1), (1, 3), (1, 2))
 ORDER = ((0, 0),) + FIRST + ((0, 2),) + SECOND
 N_SENT = (4 + 1 + 3 + 7) * PIECES
@@ -79,17 +79,18 @@
     list_v[...] = entry
     list_copy = pltpu.make_async_copy(list_v, list_s, in_sem.at[2])
     list_copy.start()
-    list_copy.wait()
+    own = jnp.broadcast_to(pltpu.roll(entry, lax.rem(256 - col * GROUP, 256), 1)[:, :1], (8, 128)) & 15
     t_copy.wait()
 
     left = lax.broadcasted_iota(jnp.int32, (64, 128), 1) < TILE
     for p in range(LIVE // 2):
         halves = []
         for h in (0, 1):
-            at = list_s[2 * p + h, col * GROUP] & 15
-            block = t_in[:, pl.ds((at >> 1) * 128, 128)]
-            odd = jnp.full((64, 128), at, jnp.int32) & 1
-            halves.append(jnp.where(odd != h, pltpu.roll(block, TILE, 1), block))
+            at = own[2 * p + h:2 * p + h + 1]
+            block = t_in[:, 7 * 128:]
+            for b in range(p, 7):
+                block = jnp.where(at >> 1 == b, t_in[:, b * 128:(b + 1) * 128], block)
+            halves.append(jnp.where(at & 1 != h, pltpu.roll(block, TILE, 1), block))
         t_all[col, p // 2, :, (p % 2) * 128:(p % 2) * 128 + 128] = jnp.where(left, halves[0], halves[1])
 
     pl.semaphore_wait(barrier, 8)
@@ -113,7 +114,7 @@
     for p in range(PIECES):
         send(col, p, "udx")
     for p in range(PIECES):
-        send(col, p, "s2")
+        send(col, p, "s")
 
     def tell(n):
         for to in near:
@@ -162,6 +163,7 @@
         multiply(e, 1)
 
     acc[...] = jnp.zeros_like(acc)
+    list_copy.wait()
     prepare((0, 0), 0)
     prepare((0, 0), 1)
     multiply((0, 0), 0)
@@ -173,7 +175,13 @@
     tell(1)
     for p in range(PIECES):
         for e in FIRST:
-            pass_on(e, p)
+            arrive(e, 0, p)
+            if e != (1, 0):
+                send(owner[e, 0], p, "x")
+        send(col, p, "2")
+        send(owner[(1, 0), 0], p, "2")
+        for e in FIRST:
+            send(owner[e, 0], p, "s")
     for e in ((0, 2),) + SECOND[:2]:
         prepare(e, 0)
         prepare(e, 1)

time: 35.1 us -> 32.6 us (0.929)
  Pallas kernels: 33.4 us -> 30.8 us
    pallas_call x1, Pallas kernels: 33.4 us -> 30.8 us  [per_device(): pl.pallas_call(functools.partial(kernel, rows), out_shape=jax.ShapeDtypeS...]
where the time goes in v3:
time: 32.6 us; the launch traced here: 32.3 us
  Pallas kernels  30.8 us (94%)
  local copies, waits for them, and re-layouts  1.47 us (5%)
    pallas_call x1, Pallas kernels, per_device(): pl.pallas_call(functools.partial(kernel, rows), out_shape=jax.ShapeDtypeS...  30.8 us
    unnamed x1, local copies, waits for them, and re-layouts  1.47 us

profile of v3, /device:TPU:0, one launch (start us, length us, event | category | flops | bytes accessed | tf_op | source)
XLA Modules:
  0.0 32.3 jit_solution(7826507462923451455)
XLA Ops:
  0.0 30.8 %shard_map.37 = f32[64,256]{1,0:T(8,128)} custom-call(f32[64,1024]{1,0:T(8,128)} %t_hbm.1, f32[16384,256]{1,0:T(8,128)} %v_hbm.1, s32[64,2048]{1,0:T(8,128)} %bitcast.1), custom_call_target="tpu_custom_call" | custom-call | tf_op jit(solution)/shard_map/pallas_call | solution.py:247
  30.8 1.5 %copy.5 = f32[64,256]{1,0:T(8,128)} copy(f32[64,256]{1,0:T(8,128)} %shard_map.37) | data formatting | bytes 131072

commit v4 on v3

--- a/solution.py
+++ b/solution.py
@@ -11,19 +11,20 @@
 GROUP = 16
 LIVE = 8
 PIECES = 2
-WIDTH = 256
+ROWS = (0, 24, 64)
 MESH = pl.DeviceIdType.MESH
 
-TREE = {(0, 1): "xs", (0, 3): "xs", (1, 0): "2s", (0, 2): "s", (1, 1): "s", (1, 3): "s", (1, 2): "s"}
+TREES = ({(0, 0): "udx", (0, 1): "xu", (0, 3): "x", (1, 0): "2"}, {(0, 0): "udx", (0, 3): "xd", (1, 0): "u2"})
 FIRST = ((0, 1), (0, 3), (1, 0))
 SECOND = ((1, 1), (1, 3), (1, 2))
-ORDER = ((0, 0),) + FIRST + ((0, 2),) + SECOND
-N_SENT = (4 + 1 + 3 + 7) * PIECES
+LATE = ((0, 2), (1, 1), (1, 3), (1, 2))
+ORDER = ((0, 0),) + FIRST + LATE
+N_SENT = 15 * PIECES
 ROUNDS = 3
 
 
-def kernel(rows, t_hbm, v_hbm, m_hbm, o_ref, t_in, m_in, list_v, list_s, v_hi, v_lo, t_all, acc, red, fin,
-           in_sem, v_sem, out_sem, got_sem, red_out, red_got, fin_out, fin_got, near_sem, *v_in):
+def kernel(rows, t_hbm, v_hbm, m_hbm, o_ref, t_in, m_in, list_v, list_s, v_hi, v_lo, t_all, acc, red,
+           in_sem, v_sem, out_sem, got_sem, red_out, red_got, near_sem, *v_in):
     row = lax.axis_index("row")
     col = lax.axis_index("col")
     core = lax.rem(col, 2)
@@ -91,15 +92,18 @@
             for b in range(p, 7):
                 block = jnp.where(at >> 1 == b, t_in[:, b * 128:(b + 1) * 128], block)
             halves.append(jnp.where(at & 1 != h, pltpu.roll(block, TILE, 1), block))
-        t_all[col, p // 2, :, (p % 2) * 128:(p % 2) * 128 + 128] = jnp.where(left, halves[0], halves[1])
+        t_all[col, :, p * 128:p * 128 + 128] = jnp.where(left, halves[0], halves[1])
 
     pl.semaphore_wait(barrier, 8)
 
     sent = []
+
+    def part(p):
+        return pl.ds(ROWS[p], ROWS[p + 1] - ROWS[p])
 
     def piece(s, p, to, n):
         return pltpu.make_async_remote_copy(
-            src_ref=t_all.at[s, p], dst_ref=t_all.at[s, p], send_sem=out_sem.at[n],
+            src_ref=t_all.at[s, part(p)], dst_ref=t_all.at[s, part(p)], send_sem=out_sem.at[n],
             recv_sem=got_sem.at[s * PIECES + p], device_id={"col": to}, device_id_type=MESH)
 
     def send(s, p, ways):
@@ -110,6 +114,9 @@
 
     def arrive(e, dc, p):
         piece(owner[e, dc], p, link["s"], 0).wait_recv()
+
+    def ways(e, p, which):
+        return "".join(w for w in TREES[p % len(TREES)].get(e, "") if w in which)
 
     for p in range(PIECES):
         send(col, p, "udx")
@@ -144,30 +151,32 @@
 
         lax.fori_loop(0, LIVE, one, 0)
 
-    def multiply(e, dc):
+    def multiply(e, dc, p):
         s = owner[e, dc]
-        t = jnp.concatenate([t_all[s, p] for p in range(PIECES)], axis=1)
+        t = t_all[s, part(p), :]
         high = t.astype(jnp.bfloat16)
         low = (t - high.astype(jnp.float32)).astype(jnp.bfloat16)
         both = jnp.dot(jnp.concatenate([high, low], axis=0), v_hi[s], preferred_element_type=jnp.float32)
         more = jnp.dot(high, v_lo[s], preferred_element_type=jnp.float32)
-        acc[...] += both[:64] + (both[64:] + more)
+        n = t.shape[0]
+        acc[part(p), :] += both[:n] + (both[n:] + more)
 
     def pass_on(e, p):
         arrive(e, 0, p)
-        send(owner[e, 0], p, TREE[e])
-
-    def sibling(e):
-        for p in range(PIECES):
-            arrive(e, 1, p)
-        multiply(e, 1)
+        send(owner[e, 0], p, ways(e, p, "ud") + "s")
+
+    def sibling(e, p):
+        arrive(e, 1, p)
+        multiply(e, 1, p)
 
     acc[...] = jnp.zeros_like(acc)
     list_copy.wait()
     prepare((0, 0), 0)
     prepare((0, 0), 1)
-    multiply((0, 0), 0)
-    sibling((0, 0))
+    for p in range(PIECES):
+        multiply((0, 0), 0, p)
+    for p in range(PIECES):
+        sibling((0, 0), p)
     for e in FIRST:
         prepare(e, 0)
         prepare(e, 1)
@@ -176,70 +185,55 @@
     for p in range(PIECES):
         for e in FIRST:
             arrive(e, 0, p)
-            if e != (1, 0):
-                send(owner[e, 0], p, "x")
-        send(col, p, "2")
-        send(owner[(1, 0), 0], p, "2")
+            send(owner[e, 0], p, ways(e, p, "x"))
+            send(owner[e, 0], p, ways(e, p, "ud"))
+        send(col, p, ways((0, 0), p, "2"))
+        send(owner[(1, 0), 0], p, ways((1, 0), p, "2"))
         for e in FIRST:
             send(owner[e, 0], p, "s")
-    for e in ((0, 2),) + SECOND[:2]:
+    for e in LATE:
         prepare(e, 0)
         prepare(e, 1)
-    for p in range(PIECES):
-        pass_on((0, 2), p)
     hear(1)
     tell(2)
     for e in FIRST:
-        multiply(e, 0)
-    for e in SECOND[2:]:
-        prepare(e, 0)
-        prepare(e, 1)
+        multiply(e, 0, 0)
     for e in FIRST:
-        sibling(e)
-    multiply((0, 2), 0)
+        sibling(e, 0)
     hear(2)
-    for p in range(PIECES):
-        for e in SECOND:
+
+    red_copies = []
+
+    def add_up(k, q, p):
+        return pltpu.make_async_remote_copy(
+            src_ref=acc.at[part(p)], dst_ref=red.at[q, part(p)], send_sem=red_out.at[p, k], recv_sem=red_got.at[p, q],
+            device_id={"row": lax.rem(row + k, rows)}, device_id_type=MESH)
+
+    for p in range(PIECES):
+        for e in LATE:
             pass_on(e, p)
-    sibling((0, 2))
-    for e in SECOND:
-        multiply(e, 0)
-    for e in SECOND:
-        sibling(e)
-
-    def part(q):
-        return pl.ds(pl.multiple_of(q * 8, 8), 8)
-
-    red_copies, fin_copies = [], []
-    for k in range(1, rows):
-        to = lax.rem(row + k, rows)
-        copy = pltpu.make_async_remote_copy(
-            src_ref=acc.at[part(to)], dst_ref=red.at[k], send_sem=red_out.at[k], recv_sem=red_got.at[k],
-            device_id={"row": to}, device_id_type=MESH)
-        copy.start()
-        red_copies.append(copy)
-    total = acc[part(row), :]
-    for copy in red_copies:
-        copy.wait_recv()
-    for k in range(1, rows):
-        total = total + red[k]
-    fin[row] = total
-    for k in range(1, rows):
-        to = lax.rem(row + k, rows)
-        copy = pltpu.make_async_remote_copy(
-            src_ref=fin.at[row], dst_ref=fin.at[row], send_sem=fin_out.at[k], recv_sem=fin_got.at[row],
-            device_id={"row": to}, device_id_type=MESH)
-        copy.start()
-        fin_copies.append(copy)
-    o_ref[part(row), :] = total
-    for k in range(1, rows):
-        q = lax.rem(row + k, rows)
-        pltpu.make_async_remote_copy(
-            src_ref=fin.at[q], dst_ref=fin.at[q], send_sem=fin_out.at[k], recv_sem=fin_got.at[q],
-            device_id={"row": q}, device_id_type=MESH).wait_recv()
-        o_ref[part(q), :] = fin[q]
-
-    for copy in sent + red_copies + fin_copies:
+        if p > 0:
+            for e in FIRST:
+                multiply(e, 0, p)
+            for e in FIRST:
+                sibling(e, p)
+        for e in LATE:
+            multiply(e, 0, p)
+        for e in LATE:
+            sibling(e, p)
+        for k in range(1, rows):
+            copy = add_up(k, row, p)
+            copy.start()
+            red_copies.append(copy)
+        red[row, part(p), :] = acc[part(p), :]
+    for p in range(PIECES):
+        for k in range(1, rows):
+            add_up(k, lax.rem(row + k, rows), p).wait_recv()
+        total = red[0, part(p), :]
+        for q in range(1, rows):
+            total = total + red[q, part(p), :]
+        o_ref[part(p), :] = total
+    for copy in sent + red_copies:
         copy.wait_send()
 
 
@@ -256,18 +250,15 @@
             pltpu.SMEM((8, 256), jnp.int32),
             pltpu.VMEM((16, LIVE * TILE, 256), jnp.bfloat16),
             pltpu.VMEM((16, LIVE * TILE, 256), jnp.bfloat16),
-            pltpu.VMEM((16, PIECES, 64, WIDTH), jnp.float32),
+            pltpu.VMEM((16, 64, 512), jnp.float32),
             pltpu.VMEM((64, 256), jnp.float32),
-            pltpu.VMEM((rows, 8, 256), jnp.float32),
-            pltpu.VMEM((rows, 8, 256), jnp.float32),
+            pltpu.VMEM((rows, 64, 256), jnp.float32),
             pltpu.SemaphoreType.DMA((3,)),
             pltpu.SemaphoreType.DMA((16,)),
             pltpu.SemaphoreType.DMA((N_SENT,)),
             pltpu.SemaphoreType.DMA((16 * PIECES,)),
-            pltpu.SemaphoreType.DMA((rows,)),
-            pltpu.SemaphoreType.DMA((rows,)),
-            pltpu.SemaphoreType.DMA((rows,)),
-            pltpu.SemaphoreType.DMA((rows,)),
+            pltpu.SemaphoreType.DMA((PIECES, rows)),
+            pltpu.SemaphoreType.DMA((PIECES, rows)),
             pltpu.SemaphoreType.REGULAR((ROUNDS,)),
         ] + [pltpu.VMEM((1024, 256), jnp.float32)] * 16,
         compiler_params=pltpu.CompilerParams(

time: 32.6 us -> 29.5 us (0.905)
  Pallas kernels: 30.8 us -> 27.8 us
    pallas_call x1, Pallas kernels: 30.8 us -> 27.8 us  [per_device(): pl.pallas_call(functools.partial(kernel, rows), out_shape=jax.ShapeDtypeS...]
where the time goes in v4:
time: 29.5 us; the launch traced here: 29.3 us
  Pallas kernels  27.8 us (94%)
  local copies, waits for them, and re-layouts  1.47 us (5%)
    pallas_call x1, Pallas kernels, per_device(): pl.pallas_call(functools.partial(kernel, rows), out_shape=jax.ShapeDtypeS...  27.8 us
    unnamed x1, local copies, waits for them, and re-layouts  1.47 us

profile of v4, /device:TPU:0, one launch (start us, length us, event | category | flops | bytes accessed | tf_op | source)
XLA Modules:
  0.0 29.3 jit_solution(13902099739536741005)
XLA Ops:
  0.0 27.8 %shard_map.37 = f32[64,256]{1,0:T(8,128)} custom-call(f32[64,1024]{1,0:T(8,128)} %t_hbm.1, f32[16384,256]{1,0:T(8,128)} %v_hbm.1, s32[64,2048]{1,0:T(8,128)} %bitcast.1), custom_call_target="tpu_custom_call" | custom-call | tf_op jit(solution)/shard_map/pallas_call | solution.py:241
  27.9 1.5 %copy.5 = f32[64,256]{1,0:T(8,128)} copy(f32[64,256]{1,0:T(8,128)} %shard_map.37) | data formatting | bytes 131072

commit v5 on v4

--- a/solution.py
+++ b/solution.py
@@ -11,7 +11,7 @@
 GROUP = 16
 LIVE = 8
 PIECES = 2
-ROWS = (0, 24, 64)
+ROWS = (0, 32, 64)
 MESH = pl.DeviceIdType.MESH
 
 TREES = ({(0, 0): "udx", (0, 1): "xu", (0, 3): "x", (1, 0): "2"}, {(0, 0): "udx", (0, 3): "xd", (1, 0): "u2"})
@@ -23,8 +23,8 @@
 ROUNDS = 3
 
 
-def kernel(rows, t_hbm, v_hbm, m_hbm, o_ref, t_in, m_in, list_v, list_s, v_hi, v_lo, t_all, acc, red,
-           in_sem, v_sem, out_sem, got_sem, red_out, red_got, near_sem, *v_in):
+def kernel(rows, t_hbm, v_hbm, m_hbm, o_ref, t_in, m_in, list_v, list_s, v_hi, v_lo, t_all, acc, sum_y, sum_x, sum_all,
+           in_sem, v_sem, out_sem, got_sem, y_out, y_got, x_out, x_got, all_out, all_got, near_sem, *v_in):
     row = lax.axis_index("row")
     col = lax.axis_index("col")
     core = lax.rem(col, 2)
@@ -83,23 +83,23 @@
     own = jnp.broadcast_to(pltpu.roll(entry, lax.rem(256 - col * GROUP, 256), 1)[:, :1], (8, 128)) & 15
     t_copy.wait()
 
-    left = lax.broadcasted_iota(jnp.int32, (64, 128), 1) < TILE
-    for p in range(LIVE // 2):
-        halves = []
-        for h in (0, 1):
-            at = own[2 * p + h:2 * p + h + 1]
-            block = t_in[:, 7 * 128:]
-            for b in range(p, 7):
-                block = jnp.where(at >> 1 == b, t_in[:, b * 128:(b + 1) * 128], block)
-            halves.append(jnp.where(at & 1 != h, pltpu.roll(block, TILE, 1), block))
-        t_all[col, :, p * 128:p * 128 + 128] = jnp.where(left, halves[0], halves[1])
-
-    pl.semaphore_wait(barrier, 8)
-
     sent = []
 
     def part(p):
         return pl.ds(ROWS[p], ROWS[p + 1] - ROWS[p])
+
+    left = lax.broadcasted_iota(jnp.int32, (1, 128), 1) < TILE
+
+    def pack(p):
+        for n in range(LIVE // 2):
+            halves = []
+            for h in (0, 1):
+                at = own[2 * n + h:2 * n + h + 1]
+                block = t_in[part(p), 7 * 128:]
+                for b in range(n, 7):
+                    block = jnp.where(at >> 1 == b, t_in[part(p), b * 128:(b + 1) * 128], block)
+                halves.append(jnp.where(at & 1 != h, pltpu.roll(block, TILE, 1), block))
+            t_all[col, part(p), n * 128:n * 128 + 128] = jnp.where(left, halves[0], halves[1])
 
     def piece(s, p, to, n):
         return pltpu.make_async_remote_copy(
@@ -118,8 +118,11 @@
     def ways(e, p, which):
         return "".join(w for w in TREES[p % len(TREES)].get(e, "") if w in which)
 
-    for p in range(PIECES):
-        send(col, p, "udx")
+    pack(0)
+    pl.semaphore_wait(barrier, 8)
+    send(col, 0, "udx")
+    pack(1)
+    send(col, 1, "udx")
     for p in range(PIECES):
         send(col, p, "s")
 
@@ -187,7 +190,6 @@
             arrive(e, 0, p)
             send(owner[e, 0], p, ways(e, p, "x"))
             send(owner[e, 0], p, ways(e, p, "ud"))
-        send(col, p, ways((0, 0), p, "2"))
         send(owner[(1, 0), 0], p, ways((1, 0), p, "2"))
         for e in FIRST:
             send(owner[e, 0], p, "s")
@@ -202,39 +204,67 @@
         sibling(e, 0)
     hear(2)
 
-    red_copies = []
-
-    def add_up(k, q, p):
+    def over_y(k, at, q):
         return pltpu.make_async_remote_copy(
-            src_ref=acc.at[part(p)], dst_ref=red.at[q, part(p)], send_sem=red_out.at[p, k], recv_sem=red_got.at[p, q],
-            device_id={"row": lax.rem(row + k, rows)}, device_id_type=MESH)
-
-    for p in range(PIECES):
-        for e in LATE:
-            pass_on(e, p)
-        if p > 0:
-            for e in FIRST:
-                multiply(e, 0, p)
-            for e in FIRST:
-                sibling(e, p)
-        for e in LATE:
-            multiply(e, 0, p)
-        for e in LATE:
-            sibling(e, p)
-        for k in range(1, rows):
-            copy = add_up(k, row, p)
-            copy.start()
-            red_copies.append(copy)
-        red[row, part(p), :] = acc[part(p), :]
-    for p in range(PIECES):
-        for k in range(1, rows):
-            add_up(k, lax.rem(row + k, rows), p).wait_recv()
-        total = red[0, part(p), :]
-        for q in range(1, rows):
-            total = total + red[q, part(p), :]
-        o_ref[part(p), :] = total
-    for copy in sent + red_copies:
+            src_ref=acc.at[part(0)], dst_ref=sum_y.at[at], send_sem=y_out.at[k], recv_sem=y_got.at[at],
+            device_id={"row": q}, device_id_type=MESH)
+
+    def over_x(at):
+        return pltpu.make_async_remote_copy(
+            src_ref=sum_x.at[at], dst_ref=sum_x.at[at], send_sem=x_out.at[0], recv_sem=x_got.at[at],
+            device_id={"row": row_of(0, 1)}, device_id_type=MESH)
+
+    def over_all(k, at, q):
+        return pltpu.make_async_remote_copy(
+            src_ref=acc.at[part(1)], dst_ref=sum_all.at[at], send_sem=all_out.at[k], recv_sem=all_got.at[at],
+            device_id={"row": q}, device_id_type=MESH)
+
+    sums = [over_y(k, y, row_of(k, 0)) for k in range(1, 4)]
+    for e in LATE:
+        pass_on(e, 0)
+    for e in LATE:
+        multiply(e, 0, 0)
+    for e in LATE:
+        sibling(e, 0)
+    for copy in sums:
+        copy.start()
+    sum_y[y] = acc[part(0), :]
+    for e in LATE:
+        pass_on(e, 1)
+    for e in FIRST:
+        multiply(e, 0, 1)
+    for e in FIRST:
+        sibling(e, 1)
+    for e in LATE:
+        multiply(e, 0, 1)
+    for e in LATE:
+        sibling(e, 1)
+    far = ((2, 1), (1, 1), (3, 1), (2, 0), (0, 1), (1, 0), (3, 0))
+    last = [over_all(k, row, row_of(*far[k - 1])) for k in range(1, rows)]
+    for copy in last:
+        copy.start()
+    sum_all[row] = acc[part(1), :]
+    for copy in sent + sums:
         copy.wait_send()
+
+    for k in range(1, 4):
+        over_y(k, lax.rem(y + k, 4), row_of(k, 0)).wait_recv()
+    sum_x[x_hi] = (sum_y[0] + sum_y[1]) + (sum_y[2] + sum_y[3])
+    across = over_x(x_hi)
+    across.start()
+    for copy in last:
+        copy.wait_send()
+    for k in range(1, rows):
+        q = lax.rem(row + k, rows)
+        over_all(k, q, q).wait_recv()
+    total = sum_all[0]
+    for q in range(1, rows):
+        total = total + sum_all[q]
+    o_ref[part(1), :] = total
+    over_x(1 - x_hi).wait_recv()
+    o_ref[part(0), :] = sum_x[0] + sum_x[1]
+    copy = across
+    copy.wait_send()
 
 
 def per_device(rows, amplitudes, ladder_ints, tile_mask):
@@ -252,13 +282,19 @@
             pltpu.VMEM((16, LIVE * TILE, 256), jnp.bfloat16),
             pltpu.VMEM((16, 64, 512), jnp.float32),
             pltpu.VMEM((64, 256), jnp.float32),
-            pltpu.VMEM((rows, 64, 256), jnp.float32),
+            pltpu.VMEM((4, ROWS[1], 256), jnp.float32),
+            pltpu.VMEM((2, ROWS[1], 256), jnp.float32),
+            pltpu.VMEM((rows, 64 - ROWS[1], 256), jnp.float32),
             pltpu.SemaphoreType.DMA((3,)),
             pltpu.SemaphoreType.DMA((16,)),
             pltpu.SemaphoreType.DMA((N_SENT,)),
             pltpu.SemaphoreType.DMA((16 * PIECES,)),
-            pltpu.SemaphoreType.DMA((PIECES, rows)),
-            pltpu.SemaphoreType.DMA((PIECES, rows)),
+            pltpu.SemaphoreType.DMA((4,)),
+            pltpu.SemaphoreType.DMA((4,)),
+            pltpu.SemaphoreType.DMA((1,)),
+            pltpu.SemaphoreType.DMA((2,)),
+            pltpu.SemaphoreType.DMA((rows,)),
+            pltpu.SemaphoreType.DMA((rows,)),
             pltpu.SemaphoreType.REGULAR((ROUNDS,)),
         ] + [pltpu.VMEM((1024, 256), jnp.float32)] * 16,
         compiler_params=pltpu.CompilerParams(

time: 29.5 us -> 29.1 us (0.986)
  Pallas kernels: 27.8 us -> 27.5 us
    pallas_call x1, Pallas kernels: 27.8 us -> 27.5 us  [per_device(): pl.pallas_call(functools.partial(kernel, rows), out_shape=jax.ShapeDtypeS...]
where the time goes in v5:
time: 29.1 us; the launch traced here: 29 us
  Pallas kernels  27.5 us (95%)
  local copies, waits for them, and re-layouts  1.47 us (5%)
    pallas_call x1, Pallas kernels, per_device(): pl.pallas_call(functools.partial(kernel, rows), out_shape=jax.ShapeDtypeS...  27.5 us
    unnamed x1, local copies, waits for them, and re-layouts  1.47 us

profile of v5, /device:TPU:0, one launch (start us, length us, event | category | flops | bytes accessed | tf_op | source)
XLA Modules:
  0.0 29.0 jit_solution(1838067370709795573)
XLA Ops:
  0.0 27.5 %shard_map.37 = f32[64,256]{1,0:T(8,128)} custom-call(f32[64,1024]{1,0:T(8,128)} %t_hbm.1, f32[16384,256]{1,0:T(8,128)} %v_hbm.1, s32[64,2048]{1,0:T(8,128)} %bitcast.1), custom_call_target="tpu_custom_call" | custom-call | tf_op jit(solution)/shard_map/pallas_call | solution.py:271
  27.5 1.5 %copy.5 = f32[64,256]{1,0:T(8,128)} copy(f32[64,256]{1,0:T(8,128)} %shard_map.37) | data formatting | bytes 131072

commit v6 on v5

--- a/solution.py
+++ b/solution.py
@@ -244,15 +244,12 @@
     for copy in last:
         copy.start()
     sum_all[row] = acc[part(1), :]
-    for copy in sent + sums:
-        copy.wait_send()
-
     for k in range(1, 4):
         over_y(k, lax.rem(y + k, 4), row_of(k, 0)).wait_recv()
     sum_x[x_hi] = (sum_y[0] + sum_y[1]) + (sum_y[2] + sum_y[3])
     across = over_x(x_hi)
     across.start()
-    for copy in last:
+    for copy in sent + sums + last:
         copy.wait_send()
     for k in range(1, rows):
         q = lax.rem(row + k, rows)
@@ -263,8 +260,7 @@
     o_ref[part(1), :] = total
     over_x(1 - x_hi).wait_recv()
     o_ref[part(0), :] = sum_x[0] + sum_x[1]
-    copy = across
-    copy.wait_send()
+    across.wait_send()
 
 
 def per_device(rows, amplitudes, ladder_ints, tile_mask):

time: 29.1 us -> 29.1 us (level)
  no operation moved by 1% of the time
where the time goes in v6:
time: 29.1 us; the launch traced here: 29 us
  Pallas kernels  27.5 us (95%)
  local copies, waits for them, and re-layouts  1.47 us (5%)
    pallas_call x1, Pallas kernels, per_device(): pl.pallas_call(functools.partial(kernel, rows), out_shape=jax.ShapeDtypeS...  27.5 us
    unnamed x1, local copies, waits for them, and re-layouts  1.47 us

profile of v6, /device:TPU:0, one launch (start us, length us, event | category | flops | bytes accessed | tf_op | source)
XLA Modules:
  0.0 29.0 jit_solution(255727915978267605)
XLA Ops:
  0.0 27.5 %shard_map.37 = f32[64,256]{1,0:T(8,128)} custom-call(f32[64,1024]{1,0:T(8,128)} %t_hbm.1, f32[16384,256]{1,0:T(8,128)} %v_hbm.1, s32[64,2048]{1,0:T(8,128)} %bitcast.1), custom_call_target="tpu_custom_call" | custom-call | tf_op jit(solution)/shard_map/pallas_call | solution.py:267
  27.5 1.5 %copy.5 = f32[64,256]{1,0:T(8,128)} copy(f32[64,256]{1,0:T(8,128)} %shard_map.37) | data formatting | bytes 131072

commit v7 on v6

--- a/solution.py
+++ b/solution.py
@@ -251,12 +251,12 @@
     across.start()
     for copy in sent + sums + last:
         copy.wait_send()
-    for k in range(1, rows):
-        q = lax.rem(row + k, rows)
-        over_all(k, q, q).wait_recv()
-    total = sum_all[0]
-    for q in range(1, rows):
-        total = total + sum_all[q]
+    total = None
+    for q in range(rows):
+        @pl.when(row != q)
+        def _():
+            over_all(1, q, q).wait_recv()
+        total = sum_all[q] if total is None else total + sum_all[q]
     o_ref[part(1), :] = total
     over_x(1 - x_hi).wait_recv()
     o_ref[part(0), :] = sum_x[0] + sum_x[1]

time: 29.1 us -> 29.1 us (level)
  no operation moved by 1% of the time
where the time goes in v7:
time: 29.1 us; the launch traced here: 29 us
  Pallas kernels  27.5 us (95%)
  local copies, waits for them, and re-layouts  1.47 us (5%)
    pallas_call x1, Pallas kernels, per_device(): pl.pallas_call(functools.partial(kernel, rows), out_shape=jax.ShapeDtypeS...  27.5 us
    unnamed x1, local copies, waits for them, and re-layouts  1.47 us

profile of v7, /device:TPU:0, one launch (start us, length us, event | category | flops | bytes accessed | tf_op | source)
XLA Modules:
  0.0 29.0 jit_solution(17955044004540277021)
XLA Ops:
  0.0 27.5 %shard_map.37 = f32[64,256]{1,0:T(8,128)} custom-call(f32[64,1024]{1,0:T(8,128)} %t_hbm.1, f32[16384,256]{1,0:T(8,128)} %v_hbm.1, s32[64,2048]{1,0:T(8,128)} %bitcast.1), custom_call_target="tpu_custom_call" | custom-call | tf_op jit(solution)/shard_map/pallas_call | solution.py:267
  27.5 1.5 %copy.5 = f32[64,256]{1,0:T(8,128)} copy(f32[64,256]{1,0:T(8,128)} %shard_map.37) | data formatting | bytes 131072
